TPU v7x, 1024 devices: a whole 4x4x32 slice. The times are simulated.
1024 devices in a mesh: fsdp: 128 (over z_lo, x, core), parity: 8 (over y, z_hi).
Axes of the slice: x: 4, y: 4, z: 32 (z_hi: 2, z_lo: 16; z = z_hi * 16 + z_lo), core: 2. Of those that a mesh axis runs over, the one named last changes fastest.
Arguments:
- param: float32 [8, 8388608], P('parity', 'fsdp'), may hold values from -0.3 to 0.3
- first_moment: float32 [8, 8388608], P('parity', 'fsdp'), may hold values from -0.0006 to 0.0006
- second_moment: float32 [8, 8388608], P('parity', 'fsdp'), may hold values from 1e-09 to 1e-07
- grad: bfloat16 [8, 8388608], P('parity', 'fsdp')
- saved_param: float32 [8, 8388608], P('parity', 'fsdp'), may hold values from -0.3 to 0.3
- owner: int32 [8], replicated, may hold values from 0 to 7, each once
- generator: float32 [8, 8], replicated, may hold values from -1 to 1, as said below
Outputs:
- new_param: float32 [8, 8388608], P('parity', 'fsdp')
- new_first: float32 [8, 8388608], P('parity', 'fsdp')
- new_second: float32 [8, 8388608], P('parity', 'fsdp')
- parity_rows: float32 [8, 8388608], P('parity', 'fsdp')
Inputs may be any that keep to these rules, and one draw needn't show every extreme that they name: owner is a permutation of the 8 code rows. generator[k, j] is the k-th power of a node of member j; the nodes are distinct.
All inputs are finite; a program needn't handle non-finite values.
Results may differ from a plain program's by a relative error of at most 0.0065.
Values may be sent and summed in bfloat16 or wider, within the bound.
A program may use at most 32 MiB of HBM per device.

v0:
```python
import jax
import jax.numpy as jnp
from jax import lax
from jax.sharding import PartitionSpec as P


def shards(param, first_moment, second_moment, grad, saved_param, owner, generator):
    grad_f = grad.astype(jnp.float32)
    local_sq = jnp.sum(grad_f * grad_f)
    total_sq = lax.psum(local_sq, ("fsdp", "parity"))
    norm = jnp.sqrt(total_sq)
    factor = jnp.minimum(1.0, 1.0 / (norm + 1e-06))
    clipped = grad_f * factor
    new_first = 0.9 * first_moment + 0.1 * clipped
    new_second = 0.95 * second_moment + 0.05 * clipped * clipped
    update = (
        new_first / (1.0 - 0.9**10) / (jnp.sqrt(new_second / (1.0 - 0.95**10)) + 1e-08)
        + 0.1 * param
    )
    new_param = param - 0.05 * update
    delta = (new_param - saved_param).astype(jnp.bfloat16)
    members = generator.shape[0]
    member = lax.axis_index("parity")
    series = jnp.arange(members, dtype=jnp.int32)
    pick_self = (series == member).astype(jnp.float32)
    column = jnp.dot(generator, pick_self, precision=lax.Precision.HIGHEST)
    delta_f = delta.astype(jnp.float32)
    onehot = (owner[:, None] == series[None, :]).astype(jnp.float32)
    coefs = jnp.dot(onehot, column, precision=lax.Precision.HIGHEST)
    parity_rows = lax.psum_scatter(
        coefs[:, None] * delta_f, "parity", scatter_dimension=0, tiled=True
    )
    return (new_param, new_first, new_second, parity_rows)


def solution(mesh):
    in_specs = (
        P("parity", "fsdp"),
        P("parity", "fsdp"),
        P("parity", "fsdp"),
        P("parity", "fsdp"),
        P("parity", "fsdp"),
        P(),
        P(),
    )
    out_specs = (P("parity", "fsdp"), P("parity", "fsdp"), P("parity", "fsdp"), P("parity", "fsdp"))
    return jax.shard_map(shards, mesh=mesh, in_specs=in_specs, out_specs=out_specs, check_vma=False)
```

profile of v0, /device:TPU:2, one launch (start us, length us, event | category | flops | bytes accessed | tf_op | source)
XLA Modules:
  0.0 937.3 jit_solution(17189996228990337677)
XLA Ops:
  7.2 0.0 copy-start
  7.2 0.0 all-reduce.3.cloned.1.call-start
  7.2 2.1 multiply_reduce_fusion
  9.3 167.7 %psum.7 = f32[]{:T(128)} all-reduce(f32[]{:T(128)} %multiply_reduce_fusion), channel_id=1, replica_groups=mesh['fsdp'=128,'parity'=8] {'fsdp','parity'}, use_global_device_ids=true, to_apply=%region_1.0 | all-reduce | flops 1 | bytes 8 | tf_op jit(solution)/shard_map/psum | solution.py:10
  177.8 0.0 copy-done
  177.8 0.1 convolution_bitcast_fusion
  177.9 0.9 convolution_bitcast_fusion.1
  178.8 4.1 convert_convert_fusion
  182.9 1.5 broadcast_multiply_fusion
  184.4 0.0 all-reduce.3.cloned.1.call-update
  184.4 1.3 dynamic-slice
  185.7 741.7 %all-reduce.3.cloned.1.call-done = f32[8,65536]{1,0:T(8,128)} async-done(((f32[8,65536]{1,0:T(8,128)}), f32[8,65536]{1,0:T(8,128)}) %all-reduce.3.cloned.1.call-update) | async-done | bytes 2097168
  927.4 3.1 constant_dynamic-slice_fusion
Async XLA Ops:
  7.2 170.6 %copy-start = (f32[8,8]{1,0:T(8,128)S(1)}, f32[8,8]{1,0:T(8,128)}, u32[]{:S(2)}) copy-start(f32[8,8]{1,0:T(8,128)} %param.13) | copy-start | bytes 772
  7.2 920.2 %all-reduce.3.cloned.1.call-start = ((), (), s32[]{:S(2)}) async-start(), calls=%async_computation | async-start | bytes 4194304
Sparse Core Ops, SparseCore 0:
  184.5 742.8 all-reduce.2
where the time goes:
time: 938 us; the launch traced here: 937 us
  waiting for transfers between devices  742 us (79%)
  blocking collectives  168 us (18%)
  between operations  14.8 us (2%)
    unnamed x2, waiting for transfers between devices  742 us
    psum x1, blocking collectives, shards(): total_sq = lax.psum(local_sq, ('fsdp', 'parity'))  168 us
  transfers between devices with their start and end apart: 1, of which 1 were waited for; matrix products, arithmetic and copies ran while one was open for 0% of the time, Pallas kernels for 0%

commit v1 on v0

v1 whole, which is shorter than its diff:
```python
import functools

import jax
import jax.numpy as jnp
from jax import lax
from jax.experimental import pallas as pl
from jax.experimental.pallas import tpu as pltpu
from jax.sharding import PartitionSpec as P

MESH = pl.DeviceIdType.MESH
NX, NY, NZ, NC = 4, 4, 32, 2
HALF = NZ // 2
REACH = NZ // 4
LANES = 128


def position():
    f = lax.axis_index("fsdp")
    p = lax.axis_index("parity")
    x = lax.rem(lax.div(f, NC), NX)
    z = lax.rem(p, 2) * HALF + lax.div(f, NX * NC)
    return x, lax.div(p, 2), z, lax.rem(f, NC)


def device(x, y, z, c):
    return ((lax.rem(z, HALF) * NX + x) * NC + c, y * 2 + lax.div(z, HALF))


def kernel(
    param, first, second, grad, saved, owner, gen,
    out_param, out_first, out_second, out_rows,
    g_v, p_v, m_v, v_v, s_v, np_v, nm_v, nv_v, rows_v, deltas,
    plane_buf, near_buf, far_buf,
    in_sem, out_sem, norm_send, norm_recv,
    z_send, z_recv, y_send, y_recv,
    *, chunks,
):
    x, y, z, c = position()
    me = lax.axis_index("parity")
    other = y * 2 + lax.rem(lax.axis_index("parity") + 1, 2)
    rows = p_v.shape[0]
    step = rows // chunks

    loads = [
        pltpu.make_async_copy(src, dst, in_sem.at[i])
        for i, (src, dst) in enumerate(
            ((grad, g_v), (param, p_v), (first, m_v), (second, v_v), (saved, s_v))
        )
    ]
    for load in loads:
        load.start()

    def along_z(k):
        return device(x, y, lax.rem(z + k + NZ, NZ), c)

    in_plane = NX * NY * NC
    mine = (x * NY + y) * NC + c

    def plane_device(j):
        return device(lax.div(j, NY * NC), lax.rem(lax.div(j, NC), NY), z, lax.rem(j, NC))

    barrier = pltpu.get_barrier_semaphore()

    def hail_z(i, _):
        for k in (REACH - i, i - REACH):
            pl.semaphore_signal(barrier, inc=1, device_id=along_z(k), device_id_type=MESH)
        return 0

    lax.fori_loop(0, REACH, hail_z, 0)

    def hail_plane(i, _):
        pl.semaphore_signal(
            barrier, inc=1, device_id=plane_device(lax.rem(mine + i + 1, in_plane)), device_id_type=MESH
        )
        return 0

    lax.fori_loop(0, in_plane - 1, hail_plane, 0)

    loads[0].wait()
    g = g_v[...].astype(jnp.float32)
    squares = jnp.sum(g * g, axis=0, keepdims=True)
    plane_buf[mine] = squares
    pl.semaphore_wait(barrier, 2 * REACH + in_plane - 1)

    def send_plane(i, _):
        pltpu.make_async_remote_copy(
            src_ref=plane_buf.at[mine], dst_ref=plane_buf.at[mine],
            send_sem=norm_send.at[0], recv_sem=norm_recv.at[0],
            device_id=plane_device(lax.rem(mine + i + 1, in_plane)), device_id_type=MESH,
        ).start()
        return 0

    def await_bytes(ref, sem):
        pltpu.make_async_copy(ref, ref, sem).wait()

    lax.fori_loop(0, in_plane - 1, send_plane, 0, unroll=True)
    await_bytes(plane_buf.at[pl.ds(0, in_plane - 1)], norm_recv.at[0])
    plane = jnp.sum(plane_buf[...], axis=0)

    near_buf[REACH - 1] = plane
    for k in (REACH, *(s * d for d in range(REACH - 1, 0, -1) for s in (1, -1))):
        pltpu.make_async_remote_copy(
            src_ref=near_buf.at[REACH - 1], dst_ref=near_buf.at[REACH - 1 + k],
            send_sem=norm_send.at[1], recv_sem=norm_recv.at[1],
            device_id=along_z(-k), device_id_type=MESH,
        ).start()
    await_bytes(near_buf.at[pl.ds(0, 2 * REACH - 1)], norm_recv.at[1])
    above = jnp.sum(near_buf[REACH - 1 :], axis=0)
    below = jnp.sum(near_buf[:REACH], axis=0)
    around = jnp.sum(near_buf[: 2 * REACH - 1], axis=0)
    far_buf[0] = above
    far_buf[1] = below
    for i, k in ((0, -REACH), (1, REACH)):
        pltpu.make_async_remote_copy(
            src_ref=far_buf.at[i], dst_ref=far_buf.at[2 + i],
            send_sem=norm_send.at[2], recv_sem=norm_recv.at[2],
            device_id=along_z(k), device_id_type=MESH,
        ).start()
    for load in loads[1:]:
        load.wait()
    await_bytes(far_buf.at[pl.ds(0, 2)], norm_recv.at[2])
    total = jnp.sum(around + far_buf[2] + far_buf[3], axis=1, keepdims=True)
    norm = jnp.sqrt(total)
    factor = jnp.minimum(1.0, 1.0 / (norm + 1e-6))

    scale_first = 1.0 / (1.0 - 0.9**10)
    scale_second = 1.0 / (1.0 - 0.95**10)

    def y_copy(hop, d, k, slot):
        part = deltas.at[slot, pl.ds(k * step, step)]
        return pltpu.make_async_remote_copy(
            src_ref=part, dst_ref=part,
            send_sem=y_send.at[hop, d - 1, k], recv_sem=y_recv.at[hop, d - 1, k],
            device_id=device(x, lax.rem(y + d, NY), z, c), device_id_type=MESH,
        )

    z_copies, y_copies = [], []
    for k in range(chunks):
        part = pl.ds(k * step, step)
        p = p_v[part]
        clipped = g_v[part].astype(jnp.float32) * factor
        new_first = 0.9 * m_v[part] + 0.1 * clipped
        new_second = 0.95 * v_v[part] + 0.05 * clipped * clipped
        update = new_first * scale_first / (jnp.sqrt(new_second * scale_second) + 1e-8) + 0.1 * p
        new_param = p - 0.05 * update
        np_v[part] = new_param
        nm_v[part] = new_first
        nv_v[part] = new_second
        deltas[me, part] = (new_param - s_v[part]).astype(jnp.bfloat16)
        own = deltas.at[me, part]
        z_copy = pltpu.make_async_remote_copy(
            src_ref=own, dst_ref=own, send_sem=z_send.at[k], recv_sem=z_recv.at[k],
            device_id=along_z(HALF), device_id_type=MESH,
        )
        z_copy.start()
        z_copies.append(z_copy)
    for k in range(chunks):
        for d in (2, 1, 3):
            copy = y_copy(0, d, k, me)
            copy.start()
            y_copies.append(copy)
    stores = [
        pltpu.make_async_copy(src, dst, out_sem.at[i])
        for i, (src, dst) in enumerate(
            ((np_v, out_param), (nm_v, out_first), (nv_v, out_second), (rows_v, out_rows))
        )
    ]
    for store in stores[:3]:
        store.start()

    row = owner[me]
    coefs = [gen[row, j] for j in range(2 * NY)]
    for copy in y_copies:
        copy.wait_recv()
    for k in range(chunks):
        z_copies[k].wait_recv()
        for d in (2, 1, 3):
            copy = y_copy(1, d, k, other)
            copy.start()
            y_copies.append(copy)
    for k in range(chunks):
        part = pl.ds(k * step, step)
        for d in range(3):
            y_copies[3 * chunks + 3 * k + d].wait_recv()
        acc = coefs[0] * deltas[0, part].astype(jnp.float32)
        for j in range(1, 2 * NY):
            acc += coefs[j] * deltas[j, part].astype(jnp.float32)
        rows_v[part] = acc
    stores[3].start()
    await_bytes(plane_buf.at[pl.ds(0, in_plane - 1)], norm_send.at[0])
    await_bytes(near_buf.at[pl.ds(0, 2 * REACH - 1)], norm_send.at[1])
    await_bytes(far_buf.at[pl.ds(0, 2)], norm_send.at[2])
    for copy in z_copies + y_copies:
        copy.wait_send()
    for store in stores:
        store.wait()


def shards(param, first_moment, second_moment, grad, saved_param, owner, generator):
    chunks = 4
    shape = param.shape
    rows = shape[1] // LANES
    tall = lambda a: a.reshape(rows, LANES)
    f32 = jax.ShapeDtypeStruct((rows, LANES), jnp.float32)
    big = pltpu.VMEM((rows, LANES), jnp.float32)
    dma = pltpu.SemaphoreType.DMA
    anywhere = pl.BlockSpec(memory_space=pl.ANY)
    smem = pl.BlockSpec(memory_space=pltpu.SMEM)
    outs = pl.pallas_call(
        functools.partial(kernel, chunks=chunks),
        out_shape=[f32] * 4,
        in_specs=[anywhere] * 5 + [smem] * 2,
        out_specs=[anywhere] * 4,
        scratch_shapes=[
            pltpu.VMEM((rows, LANES), grad.dtype), big, big, big, big, big, big, big, big,
            pltpu.VMEM((2 * NY, rows, LANES), jnp.bfloat16),
            pltpu.VMEM((NX * NY * NC, 1, LANES), jnp.float32),
            pltpu.VMEM((2 * REACH, 1, LANES), jnp.float32),
            pltpu.VMEM((4, 1, LANES), jnp.float32),
            dma((5,)), dma((4,)), dma((3,)), dma((3,)),
            dma((chunks,)), dma((chunks,)), dma((2, 3, chunks)), dma((2, 3, chunks)),
        ],
        compiler_params=pltpu.CompilerParams(
            collective_id=0, has_side_effects=True, vmem_limit_bytes=56 * 1024 * 1024
        ),
    )(
        tall(param), tall(first_moment), tall(second_moment), tall(grad), tall(saved_param),
        owner, generator,
    )
    return tuple(o.reshape(shape) for o in outs)


def solution(mesh):
    split = P("parity", "fsdp")
    return jax.shard_map(
        shards, mesh=mesh, in_specs=(split,) * 5 + (P(), P()), out_specs=(split,) * 4, check_vma=False
    )
```

time: 938 us -> 81.2 us (0.09)
  the two profiles are of different devices: /device:TPU:2 before, /device:TPU:256 now
where the time goes in v1:
time: 81.2 us; the launch traced here: 80.9 us
  Pallas kernels  73.4 us (90%)
  local copies, waits for them, and re-layouts  4.5 us (6%)
  other arithmetic  2.33 us (3%)
    pallas_call x1, Pallas kernels, shards(): pl.pallas_call(functools.partial(kernel, chunks=chunks), out_shape=[f32]...  73.4 us
    unnamed x10, local copies, waits for them, and re-layouts  4.5 us
    unnamed x1, other arithmetic  2.33 us

profile of v1, /device:TPU:256, one launch (start us, length us, event | category | flops | bytes accessed | tf_op | source)
XLA Modules:
  0.0 80.9 jit_solution(17819460721058960633)
XLA Ops:
  0.6 2.3 %reduce = bf16[65536]{0:T(1024)(128)(2,1)} reduce(bf16[1,65536]{1,0:T(2,128)(2,1)} %param.10, bf16[]{:T(256)} %constant.5), dimensions={0}, to_apply=%param.10.reduce_sub_computation | reduce | bytes 262146 | tf_op args[3]
  3.0 73.4 %shard_map.102 = (f32[512,128]{1,0:T(8,128)}, f32[512,128]{1,0:T(8,128)}, f32[512,128]{1,0:T(8,128)}, f32[512,128]{1,0:T(8,128)}) custom-call(f32[512,128]{1,0:T(8,128)} %bitcast.14, f32[512,128]{1,0:T(8,128)} %bitcast.15, f32[512,128]{1,0:T(8,128)} %bitcast.16, bf16[512,128]{1,0:T(8,128)(2,1)} %bitcast.9, f32[512,128]{1,0:T(8,128)} %bitcast.17, s32[8]{0:T(128)} %owner.1, ...), custom_call_target="tpu_custom_call" | custom-call | tf_op jit(solution)/shard_map/pallas_call | solution.py:209
  76.4 0.0 copy-start.2
  76.4 1.7 %copy.15 = f32[1,65536]{1,0:T(1,128)} copy(f32[1,65536]{1,0:T(1,128)} %bitcast.13) | data formatting | bytes 524288
  78.1 0.0 copy-done.2
  78.1 0.0 copy-start.1
  78.1 0.7 copy.16
  78.8 0.3 copy-done.1
  79.1 0.0 copy-start
  79.1 0.7 copy.17
  79.9 0.3 copy-done
  80.2 0.7 copy.18
Async XLA Ops:
  76.4 1.7 %copy-start.2 = (f32[512,128]{1,0:T(8,128)S(1)}, f32[512,128]{1,0:T(8,128)}, u32[]{:S(2)}) copy-start(f32[512,128]{1,0:T(8,128)} %get-tuple-element.9) | copy-start | bytes 786436
  78.1 1.0 %copy-start.1 = (f32[512,128]{1,0:T(8,128)S(1)}, f32[512,128]{1,0:T(8,128)}, u32[]{:S(2)}) copy-start(f32[512,128]{1,0:T(8,128)} %get-tuple-element.10) | copy-start | bytes 786436
  79.1 1.0 %copy-start = (f32[512,128]{1,0:T(8,128)S(1)}, f32[512,128]{1,0:T(8,128)}, u32[]{:S(2)}) copy-start(f32[512,128]{1,0:T(8,128)} %get-tuple-element.11) | copy-start | bytes 786436

commit v2 on v1

v2 whole, which is shorter than its diff:
```python
import functools

import jax
import jax.numpy as jnp
from jax import lax
from jax.experimental import pallas as pl
from jax.experimental.pallas import tpu as pltpu
from jax.sharding import PartitionSpec as P

MESH = pl.DeviceIdType.MESH
NY, NZ = 4, 32
HALF = NZ // 2
REACH = NZ // 4
STRIDE = REACH // 2
PLANE = 32
LANES = 128
CHUNKS = 4
STARTS = (
    16, 8, 8, 4, 8, 6, 9, 4, 7, 7, 6, 6, 6, 5, 8, 12,
    0, 0, 0, 3, 0, 10, 0, 16, 6, 0, 4, 12, 4, 0, 6, 13,
)


def kernel(
    param, first, second, grad, saved, owner, gen,
    out_param, out_first, out_second, out_rows,
    g_v, gf_v, p_v, m_v, v_v, s_v, np_v, nm_v, nv_v, rows_v, deltas,
    plane_buf, near_buf, far_buf,
    in_sem, out_sem, norm_send, norm_recv,
    z_send, z_recv, y_send, y_recv, known, go,
):
    f = lax.axis_index("fsdp")
    me = lax.axis_index("parity")
    z = (me & 1) * HALF + (f >> 3)
    other = me ^ 1
    rows = p_v.shape[0]
    step = rows // CHUNKS

    loads = [
        pltpu.make_async_copy(src, dst, in_sem.at[i])
        for i, (src, dst) in enumerate(
            ((grad, g_v), (param, p_v), (first, m_v), (second, v_v), (saved, s_v))
        )
    ]
    for load in loads:
        load.start()

    def along_z(k):
        t = (z + (k + NZ)) & (NZ - 1)
        return ((t & (HALF - 1)) * 8 + (f & 7), (me & 6) | (t >> 4))

    def along_y(d):
        return (f, (me + 2 * d) & 7)

    mine = (me >> 1) * 8 + (f & 7)

    def in_plane(j):
        return (f ^ (j & 7), me ^ ((j >> 3) * 2))

    def member(bits):
        word = bits - (1 << NZ) if bits >> (NZ - 1) else bits
        return ((jnp.int32(word) >> z) & 1) == 1

    def signal(sem, device):
        pl.semaphore_signal(sem, inc=1, device_id=device, device_id_type=MESH)

    def await_bytes(ref, sem):
        pltpu.make_async_copy(ref, ref, sem).wait()

    barrier = pltpu.get_barrier_semaphore()
    for k in range(STRIDE, 0, -1):
        signal(barrier, along_z(k))
        signal(barrier, along_z(-k))
    for j in range(PLANE - 1, 0, -1):
        signal(barrier, in_plane(j))

    loads[0].wait()
    g = g_v[...].astype(jnp.float32).reshape(rows, LANES)
    gf_v[...] = g
    plane_buf[mine] = jnp.sum(g * g, axis=0, keepdims=True)
    pl.semaphore_wait(barrier, 2 * STRIDE + PLANE - 1)
    for j in range(PLANE - 1, 0, -1):
        pltpu.make_async_remote_copy(
            src_ref=plane_buf.at[mine], dst_ref=plane_buf.at[mine],
            send_sem=norm_send.at[0], recv_sem=norm_recv.at[0],
            device_id=in_plane(j), device_id_type=MESH,
        ).start()
    signal(known, along_z(STRIDE))
    signal(known, along_z(-STRIDE))
    await_bytes(plane_buf.at[pl.ds(0, PLANE - 1)], norm_recv.at[0])

    near_buf[REACH - 1] = jnp.sum(plane_buf[...], axis=0)
    pl.semaphore_wait(known, 2)
    for k in (REACH, *(s * d for d in range(REACH - 1, 0, -1) for s in (1, -1))):
        pltpu.make_async_remote_copy(
            src_ref=near_buf.at[REACH - 1], dst_ref=near_buf.at[REACH - 1 + k],
            send_sem=norm_send.at[1], recv_sem=norm_recv.at[1],
            device_id=along_z(-k), device_id_type=MESH,
        ).start()
    await_bytes(near_buf.at[pl.ds(0, 2 * REACH - 1)], norm_recv.at[1])
    far_buf[0] = jnp.sum(near_buf[REACH - 1 :], axis=0)
    far_buf[1] = jnp.sum(near_buf[:REACH], axis=0)
    for i, k in ((0, -REACH), (1, REACH)):
        pltpu.make_async_remote_copy(
            src_ref=far_buf.at[i], dst_ref=far_buf.at[2 + i],
            send_sem=norm_send.at[2], recv_sem=norm_recv.at[2],
            device_id=along_z(k), device_id_type=MESH,
        ).start()
    around = jnp.sum(near_buf[: 2 * REACH - 1], axis=0)
    for load in loads[1:]:
        load.wait()
    await_bytes(far_buf.at[pl.ds(0, 2)], norm_recv.at[2])
    total = jnp.sum(around + far_buf[2] + far_buf[3], axis=1, keepdims=True)
    norm = jnp.sqrt(total)
    factor = jnp.minimum(1.0, 1.0 / (norm + 1e-6))

    def part_of(k):
        return pl.ds(k * step, step)

    def z_copy(k):
        part = deltas.at[me, part_of(k)]
        return pltpu.make_async_remote_copy(
            src_ref=part, dst_ref=part, send_sem=z_send.at[k], recv_sem=z_recv.at[k],
            device_id=along_z(HALF), device_id_type=MESH,
        )

    def y_copy(hop, d, k, slot):
        part = deltas.at[slot, part_of(k)]
        return pltpu.make_async_remote_copy(
            src_ref=part, dst_ref=part,
            send_sem=y_send.at[hop, d - 1, k], recv_sem=y_recv.at[hop, d - 1, k],
            device_id=along_y(d), device_id_type=MESH,
        )

    scale_first = 1.0 / (1.0 - 0.9**10)
    scale_second = 1.0 / (1.0 - 0.95**10)

    def adamw(k):
        part = part_of(k)
        p = p_v[part]
        clipped = gf_v[part] * factor
        new_first = 0.9 * m_v[part] + 0.1 * clipped
        new_second = 0.95 * v_v[part] + 0.05 * clipped * clipped
        update = new_first * scale_first / (jnp.sqrt(new_second * scale_second) + 1e-8) + 0.1 * p
        new_param = p - 0.05 * update
        np_v[part] = new_param
        nm_v[part] = new_first
        nv_v[part] = new_second
        deltas[me, part] = (new_param - s_v[part]).astype(jnp.bfloat16)

    for hops in sorted(set(STARTS) - {0}):
        senders = sum(1 << ((t - hops) % NZ) for t in range(NZ) if STARTS[t] == hops)

        @pl.when(member(senders))
        def _():
            signal(go, along_z(hops))

    waits = member(sum(1 << t for t in range(NZ) if STARTS[t]))
    for k in range(CHUNKS):
        adamw(k)
        pl.when(jnp.logical_not(waits))(z_copy(k).start)
    for k in range(CHUNKS):
        for d in (2, 1, 3):
            y_copy(0, d, k, me).start()
    stores = [
        pltpu.make_async_copy(src, dst, out_sem.at[i])
        for i, (src, dst) in enumerate(
            ((np_v, out_param), (nm_v, out_first), (nv_v, out_second))
        )
    ]

    def row_store(k):
        part = part_of(k)
        return pltpu.make_async_copy(rows_v.at[part], out_rows.at[part], out_sem.at[3 + k])

    for store in stores:
        store.start()

    @pl.when(waits)
    def _():
        pl.semaphore_wait(go, 1)
        for k in range(CHUNKS):
            z_copy(k).start()

    row = owner[me]
    here = [gen[row, (2 * d) + (me & 1)] for d in range(NY)]
    there = [gen[row, (2 * d) + (other & 1)] for d in range(NY)]

    def mix(coefs, half, k):
        part = part_of(k)
        return sum(coefs[d] * deltas[2 * d + half, part].astype(jnp.float32) for d in range(NY))

    for k in range(CHUNKS):
        for d in (1, 2, 3):
            y_copy(0, d, k, me).wait_recv()
        rows_v[part_of(k)] = mix(here, me & 1, k)
    for k in range(CHUNKS):
        z_copy(k).wait_recv()
        for d in (2, 1, 3):
            y_copy(1, d, k, other).start()
    for k in range(CHUNKS):
        for d in (1, 3, 2):
            y_copy(1, d, k, other).wait_recv()
        part = part_of(k)
        rows_v[part] += mix(there, other & 1, k)
        row_store(k).start()
    await_bytes(plane_buf.at[pl.ds(0, PLANE - 1)], norm_send.at[0])
    await_bytes(near_buf.at[pl.ds(0, 2 * REACH - 1)], norm_send.at[1])
    await_bytes(far_buf.at[pl.ds(0, 2)], norm_send.at[2])
    for k in range(CHUNKS):
        z_copy(k).wait_send()
        for d in (1, 2, 3):
            y_copy(0, d, k, me).wait_send()
            y_copy(1, d, k, other).wait_send()
    for store in stores:
        store.wait()
    for k in range(CHUNKS):
        row_store(k).wait()


def finish(*refs):
    for src, dst in zip(refs[:4], refs[4:]):
        dst[...] = src[...]


def shards(param, first_moment, second_moment, grad, saved_param, owner, generator):
    shape = param.shape
    rows = shape[1] // LANES

    def tall(a):
        return a.reshape(rows, LANES)

    f32 = jax.ShapeDtypeStruct((rows, LANES), jnp.float32)
    big = pltpu.VMEM((rows, LANES), jnp.float32)
    dma = pltpu.SemaphoreType.DMA
    regular = pltpu.SemaphoreType.REGULAR
    anywhere = pl.BlockSpec(memory_space=pl.ANY)
    vmem = pl.BlockSpec(memory_space=pltpu.VMEM)
    smem = pl.BlockSpec(memory_space=pltpu.SMEM)
    outs = pl.pallas_call(
        kernel,
        out_shape=[f32] * 4,
        in_specs=[anywhere] * 5 + [smem] * 2,
        out_specs=[anywhere] * 4,
        scratch_shapes=[
            pltpu.VMEM(shape, grad.dtype), *[big] * 9,
            pltpu.VMEM((2 * NY, rows, LANES), jnp.bfloat16),
            pltpu.VMEM((PLANE, 1, LANES), jnp.float32),
            pltpu.VMEM((2 * REACH, 1, LANES), jnp.float32),
            pltpu.VMEM((4, 1, LANES), jnp.float32),
            dma((5,)), dma((3 + CHUNKS,)), dma((3,)), dma((3,)),
            dma((CHUNKS,)), dma((CHUNKS,)), dma((2, 3, CHUNKS)), dma((2, 3, CHUNKS)),
            regular, regular,
        ],
        compiler_params=pltpu.CompilerParams(
            collective_id=0, has_side_effects=True, vmem_limit_bytes=56 * 1024 * 1024
        ),
    )(
        tall(param), tall(first_moment), tall(second_moment), grad, tall(saved_param),
        owner, generator,
    )
    block = pl.BlockSpec((rows // 2, LANES), lambda i: (i, 0))
    outs = pl.pallas_call(
        finish,
        out_shape=[f32] * 4,
        grid=(2,),
        in_specs=[block] * 4,
        out_specs=[block] * 4,
        compiler_params=pltpu.CompilerParams(vmem_limit_bytes=56 * 1024 * 1024),
    )(*outs)
    return tuple(o.reshape(shape) for o in outs)


def solution(mesh):
    split = P("parity", "fsdp")
    return jax.shard_map(
        shards, mesh=mesh, in_specs=(split,) * 5 + (P(), P()), out_specs=(split,) * 4, check_vma=False
    )
```

time: 81.2 us -> 74.7 us (0.920)
  the two profiles are of different devices: /device:TPU:256 before, /device:TPU:224 now
where the time goes in v2:
time: 74.7 us; the launch traced here: 74.5 us
  Pallas kernels  73.8 us (99%)
    pallas_call x1, Pallas kernels, shards(): pl.pallas_call(kernel, out_shape=[f32] * 4, in_specs=[anywhere] * 5 + [sm...  71.7 us
    pallas_call x1, Pallas kernels, shards(): pl.pallas_call(finish, out_shape=[f32] * 4, grid=(2,), in_specs=[block] *...  2.13 us

profile of v2, /device:TPU:224, one launch (start us, length us, event | category | flops | bytes accessed | tf_op | source)
XLA Modules:
  0.0 74.5 jit_solution(6902312696594987771)
XLA Ops:
  0.6 71.7 %shard_map.102 = (f32[512,128]{1,0:T(8,128)}, f32[512,128]{1,0:T(8,128)}, f32[512,128]{1,0:T(8,128)}, f32[512,128]{1,0:T(8,128)}) custom-call(f32[512,128]{1,0:T(8,128)} %bitcast.8, f32[512,128]{1,0:T(8,128)} %bitcast.9, f32[512,128]{1,0:T(8,128)} %bitcast.10, bf16[1,65536]{1,0:T(2,128)(2,1)} %grad.1, f32[512,128]{1,0:T(8,128)} %bitcast.11, s32[8]{0:T(128)} %owner.1, ...), custom_call_target="tpu_custom_call" | custom-call | tf_op jit(solution)/shard_map/pallas_call | solution.py:240
  72.3 2.1 %shard_map.103 = (f32[512,128]{1,0:T(8,128)}, f32[512,128]{1,0:T(8,128)}, f32[512,128]{1,0:T(8,128)}, f32[512,128]{1,0:T(8,128)}) custom-call(f32[512,128]{1,0:T(8,128)} %get-tuple-element.12.refs_0_, f32[512,128]{1,0:T(8,128)} %get-tuple-element.13.refs_1_, f32[512,128]{1,0:T(8,128)} %get-tuple-element.14.refs_2_, f32[512,128]{1,0:T(8,128)} %get-tuple-element.15.refs_3_), custom_call_target="tpu_custom_call" | custom-call | tf_op jit(solution)/shard_map/pallas_call | solution.py:263
